TPU v7x, 256 devices: a whole 4x4x8 slice. The times are simulated.
256 devices in a mesh: ctx: 8 (over x_lo, y), exp: 32 (over z, x_hi, core).
Axes of the slice: x: 4 (x_hi: 2, x_lo: 2; x = x_hi * 2 + x_lo), y: 4, z: 8, core: 2. Of those that a mesh axis runs over, the one named last changes fastest.
Arguments:
- hidden_in: bfloat16 [32, 1024, 2048], P('exp', 'ctx'), may hold values from -3 to 3
- query: bfloat16 [32, 1024, 4096], P('exp', 'ctx'), may hold values from -96 to 96
- keyval: bfloat16 [32, 1024, 512], P('exp', 'ctx'), may hold values from -5 to 5
- out_proj: bfloat16 [4096, 2048], P('exp'), may hold values from -0.375 to 0.375
- norm_gain: bfloat16 [2048], replicated, may hold values from 0.099609375 to 1.8984375
- expert_ids: int32 [32, 1024, 8], P('exp', 'ctx'), may hold values from 0 to 31, all different within a row; in each aligned block of 128 rows (0 to 127, 128 to 255, ..., all dimensions but the last counted through in order) at most 34 rows name the same one
- gate_weights: float32 [32, 1024, 8], P('exp', 'ctx'), may hold values from 0.1 to 0.4
- w_gate: bfloat16 [32, 2048, 768], P('exp'), may hold values from -0.125 to 0.125
- w_up: bfloat16 [32, 2048, 768], P('exp'), may hold values from -0.125 to 0.125
- w_down: bfloat16 [32, 768, 2048], P('exp'), may hold values from -0.21875 to 0.21875
Outputs:
- layer_out: bfloat16 [32, 1024, 2048], P('exp', 'ctx')
Inputs may be any that keep to these rules, and one draw needn't show every extreme that they name: `expert_ids`: in each aligned block of 128 tokens (the tokens of one device) no expert is named by more than 34 tokens, a bound that some block reaches; a token names 8 different experts.
All inputs are finite; a program needn't handle non-finite values.
Results may differ from a plain program's by a relative error of at most 0.014.
Values may be sent and summed in bfloat16 or wider, within the bound.
A program may use at most 128 MiB of HBM per device.

v0:
```python
import functools
import math

import jax
import jax.numpy as jnp
from jax import lax
from jax.experimental import pallas as pl
from jax.experimental.pallas import tpu as pltpu
from jax.sharding import PartitionSpec as P

D = 2048
QH = 32
KVH = 2
HD = 128
EF = 768
TOP = 8
TOK = 128
EXPERTS = 32
CAP = 34
ROWS = 144
HALF = 64
DIRECT = 512
QUARTER = 256
RING = DIRECT + 2 * QUARTER
SIDE = 4
NZ = 8
NCTX = 8
MESH = pl.DeviceIdType.MESH
BF = jnp.bfloat16
F32 = jnp.float32

A0, A1, B0 = 0, 1, 2
STREAM = ((0, 0), (1, 0), (0, 1))
HOPS = ((4, 3), (3, 4), (4, 3))


class Place:
    def __init__(self):
        ctx, exp = lax.axis_index("ctx"), lax.axis_index("exp")
        self.ctx, self.exp = ctx, exp
        self.xlo, self.y = ctx // 4, ctx % 4
        self.z, self.xhi, self.core = exp // 4, (exp // 2) % 2, exp % 2

    def device(self, xlo, z, xhi, core):
        return {"ctx": xlo * 4 + self.y, "exp": z * 4 + xhi * 2 + core}

    def up(self):
        return self.device(self.xlo, (self.z + 1) % NZ, self.xhi, self.core)

    def down(self):
        return self.device(self.xlo, (self.z + NZ - 1) % NZ, self.xhi, self.core)

    def cross(self):
        return self.device(1 - self.xlo, self.z, 1 - self.xhi, self.core)

    def peer(self):
        return self.device(self.xlo, self.z, self.xhi, 1 - self.core)

    def plane(self, rel):
        return (self.z + rel + NZ) % NZ

    def column(self, col):
        return self.xhi if col == 0 else 1 - self.xhi

    def slot(self, rel, col, core=None):
        core = self.core if core is None else core
        return self.plane(rel) * 4 + self.column(col) * 2 + core


def rels(k):
    return (0,) if k == 0 else ((4,) if k == 4 else (-k, k))


def remote(src, dst, send, recv, device):
    return pltpu.make_async_remote_copy(
        src_ref=src, dst_ref=dst, send_sem=send, recv_sem=recv, device_id=device, device_id_type=MESH
    )


class Gather:
    def __init__(self, at, buf, zs, zr, cs, cr, ps, pr):
        self.at, self.buf = at, buf
        self.zs, self.zr, self.cs, self.cr, self.ps, self.pr = zs, zr, cs, cr, ps, pr
        self.sent = {k: [] for k in range(5)}

    def rows(self, rel, col, half, core=None):
        start = self.at.slot(rel, col, core) * TOK + half * HALF
        return self.buf.at[pl.ds(pl.multiple_of(start, HALF), HALF)]

    def go(self, k, copy):
        copy.start()
        self.sent[k].append(copy)

    def hop(self, stream, direction, k):
        col, half = STREAM[stream]
        if k > HOPS[stream][direction]:
            return
        rel = -(k - 1) if direction == 0 else k - 1
        ref = self.rows(rel, col, half)
        to = self.at.up() if direction == 0 else self.at.down()
        self.go(abs(rel), remote(ref, ref, self.zs.at[stream, direction, k], self.zr.at[stream, direction, k], to))

    def crossing(self, rel, half):
        ref = self.rows(rel, 0, half)
        index = rel % NZ if half == 1 else NZ
        return remote(ref, ref, self.cs.at[index], self.cr.at[index], self.at.cross())

    def crossed(self, rel, half):
        ref = self.rows(rel, 1, half)
        index = rel % NZ if half == 1 else NZ
        remote(ref, ref, self.cs.at[index], self.cr.at[index], self.at.cross()).wait_recv()

    def block(self, rel, col, core=None):
        return self.buf.at[pl.ds(pl.multiple_of(self.at.slot(rel, col, core) * TOK, TOK), TOK)]

    def share(self, rel, col):
        ref = self.block(rel, col)
        index = (rel % NZ) * 2 + col
        self.go(abs(rel), remote(ref, ref, self.ps.at[index], self.pr.at[index], self.at.peer()))

    def begin(self):
        self.go(0, self.crossing(0, 0))
        for stream in (B0, A0):
            for direction in (0, 1):
                self.hop(stream, direction, 1)
        self.go(0, self.crossing(0, 1))
        self.share(0, 0)

    def begin_column(self):
        self.crossed(0, 0)
        for direction in (0, 1):
            self.hop(A1, direction, 1)

    def ring(self, k):
        for stream in (B0, A0, A1):
            col, half = STREAM[stream]
            for direction in (0, 1):
                if k > HOPS[stream][direction]:
                    continue
                rel = -k if direction == 0 else k
                rel = 4 if k == 4 else rel
                ref = self.rows(rel, col, half)
                sem = self.zr.at[stream, direction, k]
                remote(ref, ref, self.zs.at[stream, direction, k], sem, self.at.up()).wait_recv()
                self.hop(stream, direction, k + 1)
                if stream == B0:
                    self.go(k, self.crossing(rel, 1))
                if stream == A0:
                    self.share(rel, 0)

    def column(self, k):
        for rel in rels(k):
            self.crossed(rel, 1)
            self.share(rel, 1)

    def shared(self, k):
        for rel in rels(k):
            for col in (0, 1):
                ref = self.block(rel, col, 1 - self.at.core)
                index = (rel % NZ) * 2 + col
                remote(ref, ref, self.ps.at[index], self.pr.at[index], self.at.peer()).wait_recv()

    def settle(self, k):
        for copy in self.sent[k]:
            copy.wait_send()


GATHER_SEMS = [
    pltpu.SemaphoreType.DMA((3, 2, 5)),
    pltpu.SemaphoreType.DMA((3, 2, 5)),
    pltpu.SemaphoreType.DMA((9,)),
    pltpu.SemaphoreType.DMA((9,)),
    pltpu.SemaphoreType.DMA((16,)),
    pltpu.SemaphoreType.DMA((16,)),
]


class Around:
    def __init__(self, at, ring, rest, ys, yr, ps, pr):
        self.at, self.ring, self.rest = at, ring, rest
        self.ys, self.yr, self.ps, self.pr = ys, yr, ps, pr
        self.sent = []

    def device(self, off):
        if off == SIDE:
            return {"ctx": (1 - self.at.xlo) * 4 + self.at.y, "exp": self.at.exp}
        return {"ctx": self.at.xlo * 4 + (self.at.y + off) % 4, "exp": self.at.exp}

    def columns(self, off):
        if off >= SIDE:
            side = (self.at.xlo + self.at.xhi + off - SIDE) % 2
            return pl.ds(pl.multiple_of(DIRECT + side * QUARTER, QUARTER), QUARTER)
        start = DIRECT + 2 * QUARTER + (self.at.y + off) % 4 * QUARTER
        return pl.ds(pl.multiple_of(start, QUARTER), QUARTER)

    def rows(self, rel, col, core=None):
        return pl.ds(pl.multiple_of(self.at.slot(rel, col, core) * TOK, TOK), TOK)

    def copy(self, src, rel, col, off, to):
        index = (rel % NZ) * 2 + col
        dst = self.rest.at[off - 1, self.rows(rel, col)]
        return remote(src, dst, self.ys.at[index, off], self.yr.at[index, off], self.device(to))

    def go(self, copy):
        copy.start()
        self.sent.append(copy)

    def give(self, rel, col):
        src = self.ring.at[self.rows(rel, col), pl.ds(DIRECT + QUARTER, QUARTER)]
        self.go(self.copy(src, rel, col, 1, 3))
        self.go(self.copy(src, rel, col, 3, 1))
        if rel == 4:
            self.go(self.copy(src, rel, col, 2, 2))
        side = self.ring.at[self.rows(rel, col), pl.ds(DIRECT, QUARTER)]
        self.go(self.copy(side, rel, col, SIDE, SIDE))

    def arrived(self, rel, col, off):
        here = self.rest.at[off - 1, self.rows(rel, col)]
        self.copy(here, rel, col, off, 1).wait_recv()

    def forward(self, rel, col):
        self.arrived(rel, col, 1)
        self.arrived(rel, col, 3)
        if rel == 4:
            return
        off, to = (3, 1) if col == 0 else (1, 3)
        self.go(self.copy(self.rest.at[off - 1, self.rows(rel, col)], rel, col, 2, to))

    def share(self, rel, col):
        if (rel, col) != (0, 0):
            self.arrived(rel, col, 2)
            self.arrived(rel, col, SIDE)
        ref = self.rest.at[:, self.rows(rel, col)]
        index = (rel % NZ) * 2 + col
        self.go(remote(ref, ref, self.ps.at[index], self.pr.at[index], self.at.peer()))

    def shared(self, k):
        for rel in rels(k):
            for col in (0, 1):
                ref = self.rest.at[:, self.rows(rel, col, 1 - self.at.core)]
                index = (rel % NZ) * 2 + col
                remote(ref, ref, self.ps.at[index], self.pr.at[index], self.at.peer()).wait_recv()

    def settle(self):
        for copy in self.sent:
            copy.wait_send()


def attention_kernel(
    hidden_hbm, query_hbm, kv_hbm, proj_hbm, gain_ref, gates_ref,
    residual_ref, normed_ref, gates_out, cross_gates_out,
    ring, rest, heads, kvs, visible, mixed, total, hidden,
    zs, zr, cs, cr, ps, pr, ks, kr, gs, gr, ys, yr, yps, ypr, g2s, g2r, own_sem,
):
    at = Place()
    position = at.ctx
    place = pl.ds(pl.multiple_of(at.exp * TOK, TOK), TOK)
    loads = [
        (kv_hbm, kvs.at[pl.ds(pl.multiple_of(position * TOK, TOK), TOK)]),
        (proj_hbm.at[:, pl.ds(0, DIRECT)], ring.at[place, pl.ds(0, DIRECT)]),
    ]
    around = Around(at, ring, rest, ys, yr, yps, ypr)
    for off in range(6):
        if off == 0:
            to = ring.at[place, pl.ds(DIRECT + QUARTER, QUARTER)]
        elif off == SIDE:
            to = ring.at[place, pl.ds(DIRECT, QUARTER)]
        else:
            to = rest.at[off - 1 if off < SIDE else SIDE - 1, place]
        loads.append((proj_hbm.at[:, around.columns(off)], to))
    for h in range(QH):
        loads.append((query_hbm.at[:, pl.ds(h * HD, HD)], heads.at[pl.ds(h * TOK, TOK)]))
    loads.append((hidden_hbm, hidden))
    loads = [pltpu.make_async_copy(src, dst, own_sem.at[i]) for i, (src, dst) in enumerate(loads)]
    for load in loads:
        load.start()

    def gate_target(off):
        other = (at.exp + off) % EXPERTS
        other_hi = (other // 2) % 2
        return other, {"ctx": ((at.xlo + at.xhi + other_hi) % 2) * 4 + at.y, "exp": other}

    barrier = pltpu.get_barrier_semaphore()

    def greet(off, carry):
        _, device = gate_target(off)
        pl.semaphore_signal(barrier, inc=1, device_id=device, device_id_type=MESH)
        return carry

    lax.fori_loop(1, EXPERTS, greet, 0)
    for off in range(1, NCTX):
        device = {"ctx": (position + off) % NCTX, "exp": at.exp}
        pl.semaphore_signal(barrier, inc=1, device_id=device, device_id_type=MESH)

    gates_out[pl.ds(at.exp, 1)] = gates_ref[pl.ds(at.exp, 1)]

    def partner_gates(off):
        plane = (at.z + off) % NZ
        src = gates_ref.at[pl.ds(plane * 4 + (1 - at.xhi) * 2, 2)]
        to = at.device(at.xlo, plane, at.xhi, at.core)
        return remote(src, cross_gates_out.at[at.z], g2s.at[off], g2r.at[off], to)

    cross_gates_out[pl.ds(at.z, 1)] = gates_ref[pl.ds(at.z * 4 + (1 - at.xhi) * 2, 2)][None]

    @pl.when(position % 2 == 0)
    def _():
        kvs[pl.ds(pl.multiple_of((position + 1) * TOK, TOK), TOK), :] = jnp.zeros((TOK, 2 * KVH * HD), BF)

    for load in loads[:8]:
        load.wait()
    pl.semaphore_wait(barrier, EXPERTS - 1 + NCTX - 1)

    gather = Gather(at, ring, zs, zr, cs, cr, ps, pr)
    gather.begin()

    mine = kvs.at[pl.ds(pl.multiple_of(position * TOK, TOK), TOK)]

    def kv_copy(off):
        device = {"ctx": (position + off) % NCTX, "exp": at.exp}
        return remote(mine, mine, ks.at[off], kr.at[off], device)

    for off in range(1, NCTX):
        pl.when(position + off < NCTX)(lambda off=off: kv_copy(off).start())

    def send_gates(off, carry):
        other, device = gate_target(off)
        remote(gates_ref.at[other], gates_out.at[at.exp], gs.at[off], gr.at[off], device).start()
        return carry

    lax.fori_loop(1, EXPERTS, send_gates, 0)
    for off in range(1, NZ):
        partner_gates(off).start()
    gather.begin_column()
    around.share(0, 0)
    for load in loads[8:]:
        load.wait()

    def kv_arrived(off):
        ref = kvs.at[pl.ds(pl.multiple_of((position + NCTX - off) % NCTX * TOK, TOK), TOK)]
        remote(ref, ref, ks.at[off], kr.at[off], {"ctx": (position + off) % NCTX, "exp": at.exp}).wait_recv()

    scale = HD ** (-0.5) * math.log2(math.e)
    last = position // 2
    row_pos = position * TOK + lax.broadcasted_iota(jnp.int32, (2 * TOK, 2 * TOK), 0) % TOK
    key_pos = last * 2 * TOK + lax.broadcasted_iota(jnp.int32, (2 * TOK, 2 * TOK), 1)
    visible[...] = jnp.where(row_pos >= key_pos, 0.0, 1.0)

    def attend(pairs, chunk, carry):
        lane = pl.multiple_of((chunk // 8) * HD, HD)
        q = heads[pl.ds(pl.multiple_of(chunk * 2 * TOK, 2 * TOK), 2 * TOK), :]
        parts, running = [], None
        for pair in range(pairs):
            keys = kvs[pair * 2 * TOK : (pair + 1) * 2 * TOK, pl.ds(lane, HD)]
            s = lax.dot_general(q, keys, (((1,), (1,)), ((), ())), preferred_element_type=F32)
            if pair == pairs - 1:
                s = jnp.where(visible[...] == 0.0, s, -1e30)
            parts.append(s)
            top = jnp.maximum(s[:, :TOK], s[:, TOK:])
            running = top if running is None else jnp.maximum(running, top)
        row_max = jnp.max(running, axis=1, keepdims=True)
        row_sum, acc = None, None
        for pair in range(pairs):
            weight = jnp.exp2((parts[pair] - row_max) * scale)
            values = kvs[pair * 2 * TOK : (pair + 1) * 2 * TOK, pl.ds(pl.multiple_of(lane + KVH * HD, HD), HD)]
            part = jnp.dot(weight.astype(BF), values, preferred_element_type=F32)
            both = weight[:, :TOK] + weight[:, TOK:]
            acc = part if acc is None else acc + part
            row_sum = both if row_sum is None else row_sum + both
        out = (acc / jnp.sum(row_sum, axis=1, keepdims=True)).astype(BF)
        plane, side = chunk // 2, chunk % 2
        for i in range(2):
            columns = pl.ds(pl.multiple_of((side * 2 + i) * HD, HD), HD)
            mixed[plane, :, columns] = out[i * TOK : (i + 1) * TOK]
        return carry

    def some(pairs, first, end):
        lax.fori_loop(first, end, functools.partial(attend, pairs), 0)

    def attend_some(first, end):
        for pairs in range(1, NCTX // 2 + 1):
            pl.when(last == pairs - 1)(
                lambda pairs=pairs: some(pairs, first, end)
            )

    def give(k, col):
        for rel in rels(k):
            around.give(rel, col)

    def forward(k, col):
        for rel in rels(k):
            around.forward(rel, col)

    def share(k):
        for rel in rels(k):
            for col in (0, 1):
                if (rel, col) != (0, 0):
                    around.share(rel, col)

    def project(k):
        gather.shared(k)
        around.shared(k)
        for rel in rels(k):
            plane = at.plane(rel)
            rows = pl.ds(pl.multiple_of(plane * 4 * TOK, 4 * TOK), 4 * TOK)

            def tile(n, carry):
                columns = pl.ds(pl.multiple_of(n * 512, 512), 512)
                total[:, columns] += jnp.dot(mixed[plane], ring[rows, columns], preferred_element_type=F32)
                return carry

            lax.fori_loop(0, DIRECT // 512, tile, 0, unroll=True)
            for off in range(6):
                if off in (0, SIDE):
                    start = DIRECT + QUARTER if off == 0 else DIRECT
                    part = ring[rows, start : start + QUARTER]
                else:
                    part = rest[off - 1 if off < SIDE else SIDE - 1, rows, :]
                columns = around.columns(off)
                total[:, columns] += jnp.dot(mixed[plane], part, preferred_element_type=F32)

    gather.column(0)
    give(0, 1)
    gather.ring(1)
    give(1, 0)
    for off in range(1, NCTX):
        pl.when(position - off >= 0)(lambda off=off: kv_arrived(off))

    attend_some(0, 5)
    gather.column(1)
    give(1, 1)
    forward(0, 1)
    gather.ring(2)
    give(2, 0)
    forward(1, 0)
    attend_some(5, 10)
    gather.column(2)
    give(2, 1)
    forward(1, 1)
    share(0)
    gather.ring(3)
    give(3, 0)
    forward(2, 0)
    share(1)
    attend_some(10, 16)
    total[...] = hidden[...].astype(F32)
    project(0)
    gather.column(3)
    give(3, 1)
    forward(2, 1)
    project(1)
    gather.ring(4)
    give(4, 0)
    forward(3, 0)
    share(2)
    gather.column(4)
    give(4, 1)
    forward(3, 1)
    project(2)
    forward(4, 0)
    share(3)
    forward(4, 1)
    project(3)
    share(4)
    project(4)

    def norm(i, carry):
        rows = pl.ds(pl.multiple_of(i * 16, 16), 16)
        r = total[rows, :]
        inverse = lax.rsqrt(jnp.mean(r * r, axis=-1, keepdims=True) + 1e-06)
        normed_ref[rows, :] = (r * inverse * gain_ref[...].astype(F32)).astype(BF)
        residual_ref[rows, :] = r
        return carry

    lax.fori_loop(0, TOK // 16, norm, 0, unroll=4)

    def take_gates(off, carry):
        other, device = gate_target(off)
        origin = (at.exp + EXPERTS - off) % EXPERTS
        copy = remote(gates_ref.at[other], gates_out.at[origin], gs.at[off], gr.at[off], device)
        copy.wait_send()
        copy.wait_recv()
        return carry

    lax.fori_loop(1, EXPERTS, take_gates, 0)
    for off in range(1, NZ):
        ref = cross_gates_out.at[(at.z + NZ - off) % NZ]
        remote(ref, ref, g2s.at[off], g2r.at[off], at.up()).wait_recv()
        partner_gates(off).wait_send()
    for off in range(1, NCTX):
        pl.when(position + off < NCTX)(lambda off=off: kv_copy(off).wait_send())
    around.settle()
    for k in range(5):
        gather.settle(k)


class Cols:
    LEAD = (0, 256)
    LOW = (0, 1024)
    HIGH = (1024, 1024)
    LOW_REST = (256, 768)


WIDE = (Cols.LOW, Cols.HIGH)
COMPACT = (Cols.LOW_REST, Cols.HIGH)
WINDOW = 80


def block_rows(k):
    return WINDOW if k in (0, 4) else ROWS


def expert_kernel(
    normed_hbm, residual_hbm, gates_ref, cross_gates_ref, gate_hbm, up_hbm, down_hbm,
    out_ref,
    own, lead, own_peer, lead_peer, own_ring, lead_ring, lead_last,
    cross_out, cross_in, window_in, result_own, result_peer, result_in, back_in, picks, spreads,
    wg, wu, wd, picked, act, residual_ref,
    zs, zr, rzs, rzr, cs, cr, rcs, rcr, ls, lr, ps, pr, wsem,
):
    at = Place()
    core, other = at.core, 1 - at.core

    def rows(rel, which=None):
        which = core if which is None else which
        return pl.ds(pl.multiple_of(at.plane(rel) * 2 * TOK + which * TOK, TOK), TOK)

    def both(rel):
        return pl.ds(pl.multiple_of(at.plane(rel) * 2 * TOK, 2 * TOK), 2 * TOK)

    def kept(rel):
        return pl.ds(pl.multiple_of(at.plane(rel) * TOK, TOK), TOK)

    def cols(part):
        return pl.ds(part[0], part[1])

    loads = (
        (normed_hbm, own.at[rows(0)]), (gate_hbm, wg), (up_hbm, wu), (down_hbm, wd),
        (residual_hbm, residual_ref),
    )
    loads = [pltpu.make_async_copy(src, dst, wsem.at[i]) for i, (src, dst) in enumerate(loads)]
    for load in loads:
        load.start()
    barrier = pltpu.get_barrier_semaphore()
    for device in (at.up(), at.down(), at.cross(), at.peer()):
        pl.semaphore_signal(barrier, inc=1, device_id=device, device_id_type=MESH)

    before = (
        lax.broadcasted_iota(jnp.int32, (TOK, TOK), 0) < lax.broadcasted_iota(jnp.int32, (TOK, TOK), 1)
    ).astype(BF)

    def place(gate, offset):
        named = gate > 0.0
        rank = jnp.dot(named.astype(BF), before, preferred_element_type=F32)
        where = jnp.where(named, rank + jnp.asarray(offset).astype(F32), -1.0)
        return where[0:1], where.T[:, 0:1]

    def numbers(count):
        return lax.broadcasted_iota(jnp.int32, (count, TOK), 0).astype(F32)

    def numbers_across(count):
        return lax.broadcasted_iota(jnp.int32, (TOK, count), 1).astype(F32)

    def one_hot(hit):
        return jnp.where(hit, 1.0, 0.0).astype(BF)

    for k in range(5):
        for i, rel in enumerate(rels(k)):
            first, first_across = place(cross_gates_ref[at.plane(rel), 0], CAP * i)
            second, second_across = place(cross_gates_ref[at.plane(rel), 1], CAP * i + CAP * len(rels(k)))
            row = numbers(block_rows(k))
            picks[rel % NZ, : block_rows(k), :] = one_hot((row == first) | (row == second))
            row = numbers_across(block_rows(k))
            spreads[rel % NZ, :, : block_rows(k)] = one_hot((row == first_across) | (row == second_across))

    sent = {k: [] for k in range(5)}
    crossing_sent = {k: [] for k in range(5)}
    returned = []

    def go(log, copy):
        copy.start()
        log.append(copy)

    def stream_ref(stream, rel):
        return lead.at[rows(rel)] if stream == 2 else own.at[rows(rel), cols(WIDE[stream])]

    def hop(stream, direction, k):
        if k > HOPS[stream][direction]:
            return
        rel = -(k - 1) if direction == 0 else k - 1
        ref = stream_ref(stream, rel)
        to = at.up() if direction == 0 else at.down()
        go(sent[abs(rel)], remote(ref, ref, zs.at[stream, direction, k], zr.at[stream, direction, k], to))

    def share(index, src, dst, log):
        go(log, remote(src, dst, ps.at[index], pr.at[index], at.peer()))

    def shared(index, ref):
        remote(ref, ref, ps.at[index], pr.at[index], at.peer()).wait_recv()

    def cross_copy(src, dst, k, part, send, recv):
        these = (pl.ds(0, block_rows(k)), cols(COMPACT[part]))
        return remote(src.at[(k, *these)], dst.at[(k, *these)], send.at[k, part], recv.at[k, part], at.cross())

    def cross(k, part):
        start, width = COMPACT[part]

        def tile(n, carry):
            columns = pl.ds(pl.multiple_of(start + n * 256, 256), 256)
            total = None
            for rel in rels(k):
                one = jnp.dot(
                    picks[rel % NZ, : block_rows(k), :], own[rows(rel), columns], preferred_element_type=F32
                )
                total = one if total is None else total + one
            cross_out[k, : block_rows(k), columns] = total.astype(BF)
            return carry

        lax.fori_loop(0, width // 256, tile, 0)
        go(crossing_sent[k], cross_copy(cross_out, cross_in, k, part, cs, cr))

    def ring(k):
        for stream in (0, 1, 2):
            for direction in (0, 1):
                if k > HOPS[stream][direction]:
                    continue
                rel = 4 if k == 4 else (-k if direction == 0 else k)
                ref = stream_ref(stream, rel)
                remote(
                    ref, ref, zs.at[stream, direction, k], zr.at[stream, direction, k], at.up()
                ).wait_recv()
                hop(stream, direction, k + 1)
                if stream == 2:
                    share(8 + rel % NZ, lead.at[rows(rel)], lead.at[rows(rel)], sent[k])
            if stream < 2:
                cross(k, stream)
        for rel in rels(k):
            share(rel % NZ, own.at[rows(rel)], own.at[rows(rel)], sent[k])

    def window(k, which):
        start = which * 64 if block_rows(k) == ROWS else which * 0
        return pl.ds(pl.multiple_of(start, 16), WINDOW)

    def rest():
        return pl.ds(256, D - 256)

    def column(k):
        for part in (0, 1):
            cross_copy(cross_out, cross_in, k, part, cs, cr).wait_recv()
        share(16 + k, cross_in.at[k, window(k, other), rest()], window_in.at[k, :, rest()], returned)

    def gather_done(k):
        for rel in rels(k):
            shared(rel % NZ, own.at[rows(rel, other)])
            shared(8 + rel % NZ, lead.at[rows(rel, other)])
        shared(16 + k, window_in.at[k, :, rest()])
        for copy in sent[k]:
            copy.wait_send()

    def process(k):
        these = rels(k)
        pair = len(these) == 2
        mine = ROWS if pair else WINDOW
        count = mine + 2 * WINDOW
        first, second = slice(mine, mine + WINDOW), slice(mine + WINDOW, count)

        def gate(rel, col, which):
            return gates_ref[at.slot(rel, col, which)]

        own_hits, own_across, gate_mine = [], [], 0.0
        for i, rel in enumerate(these):
            hits, across = [], []
            for which in (0, 1):
                g = gate(rel, 0, which)
                line, standing = place(g, CAP * (2 * i + which))
                hit = numbers(mine) == line
                gate_mine = gate_mine + jnp.sum(jnp.where(hit, g[0:1], 0.0), axis=1, keepdims=True)
                hits.append(one_hot(hit))
                across.append(one_hot(numbers_across(mine) == standing))
            own_hits.append(jnp.concatenate(hits, axis=1))
            own_across.append(jnp.concatenate(across, axis=0))
        window_hits, window_across, gate_windows = [], [], []
        offset = 4 * core if pair else CAP * core
        for which in (core, other):
            hits, across, total = [], [], 0.0
            for i, rel in enumerate(these):
                g = gate(rel, 1, which)
                line, standing = place(g, offset + CAP * i)
                hit = numbers(WINDOW) == line
                total = total + jnp.sum(jnp.where(hit, g[0:1], 0.0), axis=1, keepdims=True)
                hits.append(one_hot(hit))
                across.append(one_hot(numbers_across(WINDOW) == standing))
            window_hits.append(hits)
            window_across.append(across)
            gate_windows.append(total)
        gate_all = jnp.concatenate([gate_mine, *gate_windows], axis=0)

        def pick(n, carry):
            columns = pl.ds(pl.multiple_of(n * 256, 256), 256)
            total = None
            for hits, rel in zip(own_hits, these):
                one = jnp.dot(hits, own[both(rel), columns], preferred_element_type=F32)
                total = one if total is None else total + one
            picked[:mine, columns] = total.astype(BF)
            return carry

        lax.fori_loop(0, D // 256, pick, 0, unroll=True)
        for side, which, target in ((0, core, first), (1, other, second)):
            total = None
            for hits, rel in zip(window_hits[side], these):
                one = jnp.dot(hits, lead[rows(rel, which), :], preferred_element_type=F32)
                total = one if total is None else total + one
            picked[target, :256] = total.astype(BF)
        picked[first, 256:] = cross_in[k, window(k, core), 256:]
        picked[second, 256:] = window_in[k, :, 256:]

        def hidden(n, carry):
            columns = pl.ds(pl.multiple_of(n * 256, 256), 256)
            x = picked[:count, :]
            g = jnp.dot(x, wg[:, columns], preferred_element_type=F32)
            u = jnp.dot(x, wu[:, columns], preferred_element_type=F32)
            act[:count, columns] = (g / (1.0 + jnp.exp(-g)) * u).astype(BF)
            return carry

        lax.fori_loop(0, EF // 256, hidden, 0, unroll=True)

        def scatter(hits, o):
            return jnp.dot(hits, o, preferred_element_type=F32).astype(BF)

        def outputs(columns):
            o = jnp.dot(act[:count, :], wd[:, columns], preferred_element_type=F32)
            o = (o * gate_all).astype(BF)
            for hits, rel in zip(own_across, these):
                own[both(rel), columns] = scatter(hits, o[:mine])
            return o

        o = outputs(slice(0, 256))
        for side, which, target in ((0, core, first), (1, other, second)):
            for hits, rel in zip(window_across[side], these):
                lead[rows(rel, which), :] = scatter(hits, o[target])

        def spread(n, carry):
            columns = pl.ds(pl.multiple_of(n * 256, 256), 256)
            o = outputs(columns)
            result_own[k, :, columns] = o[first]
            result_peer[k, :, columns] = o[second]
            return carry

        lax.fori_loop(1, D // 256, spread, 0, unroll=True)
        for rel in these:
            share(21 + rel % NZ, own.at[rows(rel, other)], own_peer.at[kept(rel)], returned)
            share(29 + rel % NZ, lead.at[rows(rel, other)], lead_peer.at[kept(rel)], returned)
        share(37 + k, result_peer.at[k, :, rest()], result_in.at[k, :, rest()], returned)

    def cross_back(k):
        for copy in crossing_sent[k]:
            copy.wait_send()
        shared(37 + k, result_in.at[k, :, rest()])

        def tile(n, carry):
            columns = pl.ds(pl.multiple_of(n * 256, 256), 256)
            if block_rows(k) == WINDOW:
                value = result_own[k, :, columns].astype(F32) + result_in[k, :, columns].astype(F32)
                cross_out[k, :WINDOW, columns] = value.astype(BF)
                return carry
            cross_out[k, window(k, core), columns] = result_own[k, :, columns]
            target = pl.ds(pl.multiple_of(80 * other, 16), 64)
            cross_out[k, target, columns] = result_in[k, pl.ds(pl.multiple_of(16 * other, 16), 64), columns]
            a = result_own[k, pl.ds(pl.multiple_of(64 * other, 16), 16), columns]
            b = result_in[k, pl.ds(pl.multiple_of(64 * core, 16), 16), columns]
            cross_out[k, 64:80, columns] = (a.astype(F32) + b.astype(F32)).astype(BF)
            return carry

        for part in (0, 1):
            start, width = COMPACT[part]
            lax.fori_loop(start // 256, (start + width) // 256, tile, 0)
            go(returned, cross_copy(cross_out, back_in, k, part, rcs, rcr))

    def ring_ref(stream, direction, k):
        if stream == 2:
            return lead_ring.at[direction * 4 + k]
        return own_ring.at[direction * 4 + k, :, cols(WIDE[stream])]

    def ring_take(stream, direction, k):
        ref = ring_ref(stream, direction, k)
        remote(
            ref, ref, rzs.at[stream, direction, k], rzr.at[stream, direction, k], at.up()
        ).wait_recv()
        return ref

    def gathered(rel, columns, with_cross, ring_parts):
        value = own[rows(rel), columns].astype(F32) + own_peer[kept(rel), columns].astype(F32)
        if with_cross:
            k = abs(rel)
            value = value + jnp.dot(
                spreads[rel % NZ, :, : block_rows(k)], back_in[k, : block_rows(k), columns],
                preferred_element_type=F32,
            )
        for slot in ring_parts:
            value = value + own_ring[slot, :, columns].astype(F32)
        return value

    def ring_give(stream, direction, k):
        if k > HOPS[stream][direction]:
            return
        rel = 4 if k == 4 else (-k if direction == 0 else k)
        chained = k + 1 <= HOPS[stream][direction]
        if chained:
            ring_take(stream, direction, k)
        slots = [direction * 4 + k] if chained else []
        if stream == 2:
            value = lead[rows(rel), :].astype(F32) + lead_peer[kept(rel), :].astype(F32)
            for slot in slots:
                value = value + lead_ring[slot].astype(F32)
            lead[rows(rel), :] = value.astype(BF)
        else:
            def tile(n, carry, with_cross=True):
                columns = pl.ds(pl.multiple_of(n * 256, 256), 256)
                own[rows(rel), columns] = gathered(rel, columns, with_cross, slots).astype(BF)
                return carry

            if stream == 0:
                tile(0, 0, False)
            lax.fori_loop(stream * 4 + (stream == 0), stream * 4 + 4, tile, 0)
        to = at.down() if direction == 0 else at.up()
        go(returned, remote(
            stream_ref(stream, rel), ring_ref(stream, direction, k - 1),
            rzs.at[stream, direction, k - 1], rzr.at[stream, direction, k - 1], to,
        ))

    def from_peer(k):
        for rel in rels(k):
            shared(21 + rel % NZ, own_peer.at[kept(rel)])
            shared(29 + rel % NZ, lead_peer.at[kept(rel)])

    loads[0].wait()
    pl.semaphore_wait(barrier, 4)
    lead_first = remote(own.at[rows(0), cols(Cols.LEAD)], lead.at[rows(0)], ls.at[0], lr.at[0], at.cross())
    go(sent[0], lead_first)
    for stream in (0, 1):
        for direction in (0, 1):
            hop(stream, direction, 1)
    share(0, own.at[rows(0)], own.at[rows(0)], sent[0])
    cross(0, 0)
    cross(0, 1)
    lead_first.wait_recv()
    for direction in (0, 1):
        hop(2, direction, 1)
    share(8, lead.at[rows(0)], lead.at[rows(0)], sent[0])

    for k in range(5):
        if k < 4:
            ring(k + 1)
        if k == 0:
            for load in loads[1:]:
                load.wait()
        column(k)
        gather_done(k)
        process(k)
        if k == 3:
            cross_back(3)

    cross_back(4)
    for k in (4, 3, 2, 1):
        from_peer(k)
        for direction in (0, 1):
            ring_give(2, direction, k)
        if k <= 3:
            cross_back(k - 1)
        for part in (0, 1):
            cross_copy(cross_out, back_in, k, part, rcs, rcr).wait_recv()
            for direction in (0, 1):
                ring_give(part, direction, k)
    from_peer(0)
    for direction in (0, 1):
        ring_take(2, direction, 0)
    value = lead[rows(0), :].astype(F32) + lead_peer[kept(0), :].astype(F32)
    lead[rows(0), :] = (value + lead_ring[0].astype(F32) + lead_ring[4].astype(F32)).astype(BF)
    last = remote(lead.at[rows(0)], lead_last, ls.at[1], lr.at[1], at.cross())
    last.start()
    for part in (0, 1):
        cross_copy(cross_out, back_in, 0, part, rcs, rcr).wait_recv()
        for direction in (0, 1):
            ring_take(part, direction, 0)

        def tile(n, carry):
            columns = pl.ds(pl.multiple_of(n * 256, 256), 256)
            value = gathered(0, columns, True, (0, 4))
            out_ref[:, columns] = (residual_ref[:, columns] + value).astype(BF)
            return carry

        lax.fori_loop(1 if part == 0 else 4, part * 4 + 4, tile, 0)
    last.wait()
    value = gathered(0, slice(0, 256), False, (0, 4)) + lead_last[...].astype(F32)
    out_ref[:, :256] = (residual_ref[:, :256] + value).astype(BF)
    for copy in returned:
        copy.wait_send()


VMEM = pl.BlockSpec(memory_space=pltpu.VMEM)
ANY = pl.BlockSpec(memory_space=pl.ANY)


def body(
    hidden_in, query, keyval, out_proj, norm_gain, expert_ids, gate_weights, w_gate, w_up, w_down
):
    names = jnp.arange(EXPERTS, dtype=jnp.int32)[:, None, None]
    gates = jnp.sum(
        jnp.where(expert_ids[0].T[None] == names, gate_weights[0].T[None], 0.0), axis=1
    )
    gates = jnp.broadcast_to(gates[:, None, :], (EXPERTS, 8, TOK))

    residual, normed, routed, cross_routed = pl.pallas_call(
        attention_kernel,
        out_shape=(
            jax.ShapeDtypeStruct((TOK, D), F32),
            jax.ShapeDtypeStruct((TOK, D), BF),
            jax.ShapeDtypeStruct((EXPERTS, 8, TOK), F32),
            jax.ShapeDtypeStruct((NZ, 2, 8, TOK), F32),
        ),
        in_specs=[ANY, ANY, ANY, ANY, VMEM, VMEM],
        out_specs=(VMEM, VMEM, VMEM, VMEM),
        scratch_shapes=[
            pltpu.VMEM((QH * HD, RING), BF),
            pltpu.VMEM((4, QH * HD, QUARTER), BF),
            pltpu.VMEM((QH * TOK, HD), BF),
            pltpu.VMEM((NCTX * TOK, 2 * KVH * HD), BF),
            pltpu.VMEM((2 * TOK, 2 * TOK), F32),
            pltpu.VMEM((NZ, TOK, 4 * HD), BF),
            pltpu.VMEM((TOK, D), F32),
            pltpu.VMEM((TOK, D), BF),
            *GATHER_SEMS,
            pltpu.SemaphoreType.DMA((NCTX,)),
            pltpu.SemaphoreType.DMA((NCTX,)),
            pltpu.SemaphoreType.DMA((EXPERTS,)),
            pltpu.SemaphoreType.DMA((EXPERTS,)),
            pltpu.SemaphoreType.DMA((16, 5)),
            pltpu.SemaphoreType.DMA((16, 5)),
            pltpu.SemaphoreType.DMA((16,)),
            pltpu.SemaphoreType.DMA((16,)),
            pltpu.SemaphoreType.DMA((NZ,)),
            pltpu.SemaphoreType.DMA((NZ,)),
            pltpu.SemaphoreType.DMA((QH + 9,)),
        ],
        compiler_params=pltpu.CompilerParams(
            collective_id=0, has_side_effects=True, vmem_limit_bytes=62 << 20
        ),
        name="attend_project",
    )(hidden_in[0], query[0], keyval[0], out_proj, norm_gain.reshape(1, D), gates)

    result = pl.pallas_call(
        expert_kernel,
        out_shape=jax.ShapeDtypeStruct((TOK, D), BF),
        in_specs=[ANY, ANY, VMEM, VMEM, ANY, ANY, ANY],
        out_specs=VMEM,
        scratch_shapes=[
            pltpu.VMEM((NZ * 2 * TOK, D), BF),
            pltpu.VMEM((NZ * 2 * TOK, 256), BF),
            pltpu.VMEM((NZ * TOK, D), BF),
            pltpu.VMEM((NZ * TOK, 256), BF),
            pltpu.VMEM((8, TOK, D), BF),
            pltpu.VMEM((8, TOK, 256), BF),
            pltpu.VMEM((TOK, 256), BF),
            pltpu.VMEM((5, ROWS, D), BF),
            pltpu.VMEM((5, ROWS, D), BF),
            pltpu.VMEM((5, WINDOW, D), BF),
            pltpu.VMEM((5, WINDOW, D), BF),
            pltpu.VMEM((5, WINDOW, D), BF),
            pltpu.VMEM((5, WINDOW, D), BF),
            pltpu.VMEM((5, ROWS, D), BF),
            pltpu.VMEM((NZ, ROWS, TOK), BF),
            pltpu.VMEM((NZ, TOK, ROWS), BF),
            pltpu.VMEM((D, EF), BF),
            pltpu.VMEM((D, EF), BF),
            pltpu.VMEM((EF, D), BF),
            pltpu.VMEM((ROWS + 2 * WINDOW, D), BF),
            pltpu.VMEM((ROWS + 2 * WINDOW, EF), BF),
            pltpu.VMEM((TOK, D), F32),
            pltpu.SemaphoreType.DMA((3, 2, 5)),
            pltpu.SemaphoreType.DMA((3, 2, 5)),
            pltpu.SemaphoreType.DMA((3, 2, 4)),
            pltpu.SemaphoreType.DMA((3, 2, 4)),
            pltpu.SemaphoreType.DMA((5, 2)),
            pltpu.SemaphoreType.DMA((5, 2)),
            pltpu.SemaphoreType.DMA((5, 2)),
            pltpu.SemaphoreType.DMA((5, 2)),
            pltpu.SemaphoreType.DMA((2,)),
            pltpu.SemaphoreType.DMA((2,)),
            pltpu.SemaphoreType.DMA((42,)),
            pltpu.SemaphoreType.DMA((42,)),
            pltpu.SemaphoreType.DMA((5,)),
        ],
        compiler_params=pltpu.CompilerParams(
            collective_id=1, has_side_effects=True, vmem_limit_bytes=62 << 20
        ),
        name="experts",
    )(normed, residual, routed, cross_routed, w_gate[0], w_up[0], w_down[0])
    return result[None]


def solution(mesh):
    in_specs = (
        P("exp", "ctx", None),
        P("exp", "ctx", None),
        P("exp", "ctx", None),
        P("exp", None),
        P(),
        P("exp", "ctx", None),
        P("exp", "ctx", None),
        P("exp", None, None),
        P("exp", None, None),
        P("exp", None, None),
    )
    out_specs = P("exp", "ctx", None)
    return jax.shard_map(body, mesh=mesh, in_specs=in_specs, out_specs=out_specs, check_vma=False)
```

profile of v0, /device:TPU:16, one launch (start us, length us, event | category | flops | bytes accessed | tf_op | source)
XLA Modules:
  0.0 212.8 jit_solution(16885021982699396381)
XLA Ops:
  0.0 1.3 reshape.6.gain_ref
  1.3 1.4 fusion.gates_ref
  2.7 72.5 %attend_project.1 = (f32[128,2048]{1,0:T(8,128)}, bf16[128,2048]{1,0:T(8,128)(2,1)}, f32[32,8,128]{2,1,0:T(8,128)}, f32[8,2,8,128]{3,2,1,0:T(8,128)}) custom-call(bf16[128,2048]{1,0:T(8,128)(2,1)} %bitcast.18, bf16[128,4096]{1,0:T(8,128)(2,1)} %bitcast.17, bf16[128,512]{1,0:T(8,128)(2,1)} %bitcast.19, bf16[128,2048]{1,0:T(8,128)(2,1)} %proj_hbm.1, ...), custom_call_target="tpu_custom_call" | custom-call | tf_op jit(solution)/shard_map/attend_project/pallas_call | solution.py:912
  75.1 135.8 %experts.1 = bf16[128,2048]{1,0:T(8,128)(2,1)} custom-call(bf16[128,2048]{1,0:T(8,128)(2,1)} %get-tuple-element.9.normed_hbm, f32[128,2048]{1,0:T(8,128)} %get-tuple-element.10.residual_hbm, f32[32,8,128]{2,1,0:T(8,128)} %get-tuple-element.11.gates_ref, f32[8,2,8,128]{3,2,1,0:T(8,128)} %get-tuple-element.12.cross_gates_ref, bf16[2048,768]{1,0:T(8,128)(2,1)} %bitcast.13, ...), custom_call_target="tpu_custom_call" | custom-call | tf_op jit(solution)/shard_map/experts/pallas_call | solution.py:950
  210.9 1.9 copy.12
where the time goes:
time: 216 us; the launch traced here: 213 us
  Pallas kernels  208 us (96%)
  local copies, waits for them, and re-layouts  3.17 us (1%)
    pallas_call x1, Pallas kernels, body(): pl.pallas_call(expert_kernel, out_shape=jax.ShapeDtypeStruct((TOK, D), BF...  136 us
    pallas_call x1, Pallas kernels, body(): pl.pallas_call(attention_kernel, out_shape=(jax.ShapeDtypeStruct((TOK, D)...  72.5 us

commit v1 on v0

--- a/solution.py
+++ b/solution.py
@@ -429,45 +429,45 @@
     gather.column(1)
     give(1, 1)
     forward(0, 1)
+    forward(1, 0)
     gather.ring(2)
     give(2, 0)
-    forward(1, 0)
+    forward(1, 1)
     attend_some(5, 10)
     gather.column(2)
     give(2, 1)
-    forward(1, 1)
+    forward(2, 0)
     share(0)
     gather.ring(3)
     give(3, 0)
-    forward(2, 0)
+    forward(2, 1)
     share(1)
     attend_some(10, 16)
     total[...] = hidden[...].astype(F32)
     project(0)
     gather.column(3)
     give(3, 1)
-    forward(2, 1)
+    forward(3, 0)
     project(1)
     gather.ring(4)
     give(4, 0)
-    forward(3, 0)
-    share(2)
+    forward(3, 1)
     gather.column(4)
     give(4, 1)
-    forward(3, 1)
+    share(2)
     project(2)
     forward(4, 0)
     share(3)
     forward(4, 1)
+    share(4)
     project(3)
-    share(4)
     project(4)
 
     def norm(i, carry):
         rows = pl.ds(pl.multiple_of(i * 16, 16), 16)
         r = total[rows, :]
         inverse = lax.rsqrt(jnp.mean(r * r, axis=-1, keepdims=True) + 1e-06)
-        normed_ref[rows, :] = (r * inverse * gain_ref[...].astype(F32)).astype(BF)
+        normed_ref[rows, :] = (r * inverse * gain_ref[...].astype(F32)[None]).astype(BF)
         residual_ref[rows, :] = r
         return carry
 
@@ -847,19 +847,22 @@
         hop(2, direction, 1)
     share(8, lead.at[rows(0)], lead.at[rows(0)], sent[0])
 
-    for k in range(5):
-        if k < 4:
-            ring(k + 1)
+    for k in range(3):
+        ring(k + 1)
         if k == 0:
             for load in loads[1:]:
                 load.wait()
         column(k)
         gather_done(k)
+        if k == 2:
+            ring(4)
         process(k)
-        if k == 3:
-            cross_back(3)
-
-    cross_back(4)
+    column(3)
+    column(4)
+    for k in (4, 3):
+        gather_done(k)
+        process(k)
+        cross_back(k)
     for k in (4, 3, 2, 1):
         from_peer(k)
         for direction in (0, 1):
@@ -945,7 +948,7 @@
             collective_id=0, has_side_effects=True, vmem_limit_bytes=62 << 20
         ),
         name="attend_project",
-    )(hidden_in[0], query[0], keyval[0], out_proj, norm_gain.reshape(1, D), gates)
+    )(hidden_in[0], query[0], keyval[0], out_proj, norm_gain, gates)
 
     result = pl.pallas_call(
         expert_kernel,

time: 216 us -> 205 us (0.949); the launches traced: 213 us -> 204 us
  Pallas kernels: 208 us -> 201 us
    pallas_call x1, Pallas kernels: 72.5 us -> 67.7 us  [body(): pl.pallas_call(attention_kernel, out_shape=(jax.ShapeDtypeStruct((TOK, D)...]
    pallas_call x1, Pallas kernels: 136 us -> 133 us  [body(): pl.pallas_call(expert_kernel, out_shape=jax.ShapeDtypeStruct((TOK, D), BF...]
where the time goes in v1:
time: 205 us; the launch traced here: 204 us
  Pallas kernels  201 us (98%)
    pallas_call x1, Pallas kernels, body(): pl.pallas_call(expert_kernel, out_shape=jax.ShapeDtypeStruct((TOK, D), BF...  133 us
    pallas_call x1, Pallas kernels, body(): pl.pallas_call(attention_kernel, out_shape=(jax.ShapeDtypeStruct((TOK, D)...  67.7 us

profile of v1, /device:TPU:16, one launch (start us, length us, event | category | flops | bytes accessed | tf_op | source)
XLA Modules:
  0.0 204.2 jit_solution(2697458059437947636)
XLA Ops:
  0.0 1.4 fusion.gates_ref
  1.4 67.7 %attend_project.1 = (f32[128,2048]{1,0:T(8,128)}, bf16[128,2048]{1,0:T(8,128)(2,1)}, f32[32,8,128]{2,1,0:T(8,128)}, f32[8,2,8,128]{3,2,1,0:T(8,128)}) custom-call(bf16[128,2048]{1,0:T(8,128)(2,1)} %bitcast.18, bf16[128,4096]{1,0:T(8,128)(2,1)} %bitcast.17, bf16[128,512]{1,0:T(8,128)(2,1)} %bitcast.19, bf16[128,2048]{1,0:T(8,128)(2,1)} %proj_hbm.1, ...), custom_call_target="tpu_custom_call" | custom-call | tf_op jit(solution)/shard_map/attend_project/pallas_call | solution.py:915
  69.1 133.2 %experts.1 = bf16[128,2048]{1,0:T(8,128)(2,1)} custom-call(bf16[128,2048]{1,0:T(8,128)(2,1)} %get-tuple-element.9.normed_hbm, f32[128,2048]{1,0:T(8,128)} %get-tuple-element.10.residual_hbm, f32[32,8,128]{2,1,0:T(8,128)} %get-tuple-element.11.gates_ref, f32[8,2,8,128]{3,2,1,0:T(8,128)} %get-tuple-element.12.cross_gates_ref, bf16[2048,768]{1,0:T(8,128)(2,1)} %bitcast.13, ...), custom_call_target="tpu_custom_call" | custom-call | tf_op jit(solution)/shard_map/experts/pallas_call | solution.py:953
  202.3 1.9 copy.12

commit v2 on v1

--- a/solution.py
+++ b/solution.py
@@ -563,7 +563,7 @@
     def one_hot(hit):
         return jnp.where(hit, 1.0, 0.0).astype(BF)
 
-    for k in range(5):
+    def prepare(k):
         for i, rel in enumerate(rels(k)):
             first, first_across = place(cross_gates_ref[at.plane(rel), 0], CAP * i)
             second, second_across = place(cross_gates_ref[at.plane(rel), 1], CAP * i + CAP * len(rels(k)))
@@ -840,12 +840,15 @@
         for direction in (0, 1):
             hop(stream, direction, 1)
     share(0, own.at[rows(0)], own.at[rows(0)], sent[0])
+    prepare(0)
     cross(0, 0)
     cross(0, 1)
     lead_first.wait_recv()
     for direction in (0, 1):
         hop(2, direction, 1)
     share(8, lead.at[rows(0)], lead.at[rows(0)], sent[0])
+    for k in range(1, 5):
+        prepare(k)
 
     for k in range(3):
         ring(k + 1)

time: 205 us -> 205 us (level)
  no operation moved by 1% of the time
where the time goes in v2:
time: 205 us; the launch traced here: 204 us
  Pallas kernels  201 us (98%)
    pallas_call x1, Pallas kernels, body(): pl.pallas_call(expert_kernel, out_shape=jax.ShapeDtypeStruct((TOK, D), BF...  133 us
    pallas_call x1, Pallas kernels, body(): pl.pallas_call(attention_kernel, out_shape=(jax.ShapeDtypeStruct((TOK, D)...  67.7 us

profile of v2, /device:TPU:16, one launch (start us, length us, event | category | flops | bytes accessed | tf_op | source)
XLA Modules:
  0.0 204.2 jit_solution(9724609759993613703)
XLA Ops:
  0.0 1.4 fusion.gates_ref
  1.4 67.7 %attend_project.1 = (f32[128,2048]{1,0:T(8,128)}, bf16[128,2048]{1,0:T(8,128)(2,1)}, f32[32,8,128]{2,1,0:T(8,128)}, f32[8,2,8,128]{3,2,1,0:T(8,128)}) custom-call(bf16[128,2048]{1,0:T(8,128)(2,1)} %bitcast.18, bf16[128,4096]{1,0:T(8,128)(2,1)} %bitcast.17, bf16[128,512]{1,0:T(8,128)(2,1)} %bitcast.19, bf16[128,2048]{1,0:T(8,128)(2,1)} %proj_hbm.1, ...), custom_call_target="tpu_custom_call" | custom-call | tf_op jit(solution)/shard_map/attend_project/pallas_call | solution.py:918
  69.1 133.2 %experts.1 = bf16[128,2048]{1,0:T(8,128)(2,1)} custom-call(bf16[128,2048]{1,0:T(8,128)(2,1)} %get-tuple-element.9.normed_hbm, f32[128,2048]{1,0:T(8,128)} %get-tuple-element.10.residual_hbm, f32[32,8,128]{2,1,0:T(8,128)} %get-tuple-element.11.gates_ref, f32[8,2,8,128]{3,2,1,0:T(8,128)} %get-tuple-element.12.cross_gates_ref, bf16[2048,768]{1,0:T(8,128)(2,1)} %bitcast.13, ...), custom_call_target="tpu_custom_call" | custom-call | tf_op jit(solution)/shard_map/experts/pallas_call | solution.py:956
  202.3 1.9 copy.12
